TPU v7x, 32 devices: a whole 2x2x4 slice. The times are simulated.
32 devices in a mesh: groups: 2 (over y), row: 8 (over z, x), col: 2 (over core).
Axes of the slice: x: 2, y: 2, z: 4, core: 2. Of those that a mesh axis runs over, the one named last changes fastest.
Arguments:
- hidden: bfloat16 [128, 14336], P(('groups', 'row'), 'col'), parts along dimension 0, may hold values from -6 to 6
- cotangent: bfloat16 [128, 8192], P(('groups', 'row')), parts along dimension 0, may hold values from -6 to 6
- weight_t: bfloat16 [8192, 14336], P('row', 'col'), may hold values from -0.0625 to 0.0625
- block_mask: int32 [32, 56], replicated, may hold values 0 or 1
Outputs:
- output: bfloat16 [128, 8192], P(('groups', 'col'), 'row'), parts along dimension 0
- weight_grad: float32 [16384, 14336], P(('groups', 'row'), 'col'), parts along dimension 0
There are 2 independent parts, one for each index of `groups`. A program takes and returns all parts, laid end to end along the dimension named above; an argument that names none is the same for every part. Nothing has to cross between parts.
All inputs are finite; a program needn't handle non-finite values.
Results may differ from a plain program's by a relative error of at most 0.001.
Values may be sent and summed in bfloat16 or wider, within the bound.
A program may use at most 128 MiB of HBM per device.

v0:
```python
import jax
import jax.numpy as jnp
from jax import lax
from jax.sharding import PartitionSpec as P

BLOCK = 256


def tile_keep(block_mask, row_start, rows, col_start, cols):
    row_ids = (row_start + jnp.arange(rows, dtype=jnp.int32)) // BLOCK
    col_ids = (col_start + jnp.arange(cols, dtype=jnp.int32)) // BLOCK
    row_pick = (
        row_ids[:, None] == jnp.arange(block_mask.shape[0], dtype=jnp.int32)[None, :]
    ).astype(jnp.bfloat16)
    col_pick = (
        jnp.arange(block_mask.shape[1], dtype=jnp.int32)[:, None] == col_ids[None, :]
    ).astype(jnp.bfloat16)
    narrow = jnp.dot(
        row_pick, block_mask.astype(jnp.bfloat16), preferred_element_type=jnp.float32
    ).astype(jnp.bfloat16)
    return jnp.dot(narrow, col_pick, preferred_element_type=jnp.float32).astype(jnp.bfloat16)


def local(hidden, cotangent, weight_t, block_mask):
    feat_rows, hid_cols = weight_t.shape
    row_index = lax.axis_index("row")
    col_index = lax.axis_index("col")
    keep = tile_keep(block_mask, row_index * feat_rows, feat_rows, col_index * hid_cols, hid_cols)
    kept = weight_t * keep
    cot_feat = lax.all_to_all(cotangent.T, "row", split_axis=0, concat_axis=1, tiled=True)
    piece = lax.all_gather(hidden, "row", axis=0, tiled=True)
    part = lax.dot_general(
        piece, kept, (((1,), (1,)), ((), ())), preferred_element_type=jnp.float32
    )
    grad = jnp.dot(cot_feat, piece, preferred_element_type=jnp.float32)
    partial_out, grad = (part, grad)
    output = lax.psum_scatter(partial_out, "col", scatter_dimension=0, tiled=True).astype(
        jnp.bfloat16
    )
    weight_grad = grad * keep.astype(jnp.float32)
    return (output, weight_grad)


def solution(mesh):
    return jax.shard_map(
        local,
        mesh=mesh,
        in_specs=(P(("groups", "row"), "col"), P(("groups", "row"), None), P("row", "col"), P()),
        out_specs=(P(("groups", "col"), "row"), P(("groups", "row"), "col")),
        check_vma=False,
    )
```

profile of v0, /device:TPU:0, one launch (start us, length us, event | category | flops | bytes accessed | tf_op | source)
XLA Modules:
  0.0 92.4 jit_solution(10172280691595588342)
XLA Ops:
  7.2 7.3 %all-to-all-start = ((bf16[8,1024,8]{1,2,0:T(8,128)(2,1)}), bf16[8,1024,8]{1,2,0:T(8,128)(2,1)S(1)}, u32[]{:S(2)}, u32[]{:S(2)}) async-start(bf16[8,1024,8]{1,2,0:T(8,128)(2,1)} %bitcast.12), calls=%async_computation.1 | async-start | bytes 262144 | tf_op jit(solution)/shard_map/all_to_all | solution.py:30
  14.4 0.0 reduce-scatter.2.cloned.1.call-start
  14.5 33.4 %all_gather.3 = bf16[64,7168]{1,0:T(8,128)(2,1)S(1)} all-gather(bf16[8,7168]{1,0:T(8,128)(2,1)} %param.4), channel_id=1, replica_groups=mesh['groups'=2,'row'=8,'col'=2] {'row'}, dimensions={0}, use_global_device_ids=true | all-gather | bytes 1032192 | tf_op jit(solution)/shard_map/all_gather | solution.py:31
  48.0 8.2 %convolution_convert_fusion = bf16[1024,7168]{1,0:T(8,128)(2,1)} fusion(s32[7168]{0:T(1024)S(1)} %add_select_fusion, s32[1024]{0:T(1024)S(1)} %add_select_fusion.1, s32[32,56]{1,0:T(8,128)} %param.7), kind=kOutput, calls=%fused_computation.3 | convolution fusion | flops 833586944 | bytes 14720000 | tf_op jit(solution)/shard_map/dot_general | solution.py:21
  56.1 12.4 %fusion.2 = f32[64,1024]{1,0:T(8,128)} fusion(bf16[64,7168]{1,0:T(8,128)(2,1)S(1)} %all_gather.3, bf16[1024,7168]{1,0:T(8,128)(2,1)} %param.6, bf16[1024,7168]{1,0:T(8,128)(2,1)} %convolution_convert_fusion), kind=kOutput, calls=%fused_computation.6 | convolution fusion | flops 946864128 | bytes 30539776 | tf_op jit(solution)/shard_map/dot_general | solution.py:32
  68.5 0.0 reduce-scatter.2.cloned.1.call-update
  68.5 0.0 all-to-all-done
  68.5 15.5 %convert_multiply_fusion = f32[1024,7168]{1,0:T(8,128)} fusion(bf16[1024,7168]{1,0:T(8,128)(2,1)} %convolution_convert_fusion, bf16[64,7168]{1,0:T(8,128)(2,1)S(1)} %all_gather.3, bf16[8,1024,8]{1,2,0:T(8,128)(2,1)S(1)} %all-to-all-done), kind=kOutput, calls=%fused_computation | convolution fusion | flops 954204160 | bytes 45088768 | tf_op jit(solution)/shard_map/dot_general | solution.py:35
  84.0 0.0 reduce-scatter.2.cloned.1.call-done
  84.0 1.5 %convert_element_type.20 = bf16[32,1024]{1,0:T(8,128)(2,1)} convert(f32[32,1024]{1,0:T(8,128)} %reduce-scatter.2.cloned.1.call-done) | non-fusion elementwise | flops 32768 | bytes 196608 | tf_op jit(solution)/shard_map/convert_element_type | solution.py:37
  (2 shorter events, 0.0 us)
Async XLA Ops:
  7.2 61.4 %all-to-all-start = ((bf16[8,1024,8]{1,2,0:T(8,128)(2,1)}), bf16[8,1024,8]{1,2,0:T(8,128)(2,1)S(1)}, u32[]{:S(2)}, u32[]{:S(2)}) async-start(bf16[8,1024,8]{1,2,0:T(8,128)(2,1)} %bitcast.12), calls=%async_computation.1 | async-start | bytes 262144 | tf_op jit(solution)/shard_map/all_to_all | solution.py:30
  14.4 69.6 %reduce-scatter.2.cloned.1.call-start = ((), (), s32[]{:S(2)}) async-start(), calls=%async_computation.2 | async-start | bytes 393216 | tf_op jit(solution)/shard_map/reduce_scatter | solution.py:37
Sparse Core Ops, SparseCore 0:
  68.7 8.3 reduce-scatter.1
where the time goes:
time: 92.8 us; the launch traced here: 92.4 us
  matrix products  36 us (39%)
  blocking collectives  33.4 us (36%)
  between operations  14.1 us (15%)
  starting transfers between devices  7.3 us (8%)
  other arithmetic  1.57 us (2%)
    all_gather x1, blocking collectives, local(): piece = lax.all_gather(hidden, 'row', axis=0, tiled=True)  33.4 us
    dot_general x1, matrix products, local(): grad = jnp.dot(cot_feat, piece, preferred_element_type=jnp.float32)  15.5 us
    dot_general x1, matrix products, local(): lax.dot_general(piece, kept, (((1,), (1,)), ((), ())), preferred_element_...  12.4 us
    dot_general x1, matrix products, tile_keep(): jnp.dot(narrow, col_pick, preferred_element_type=jnp.float32)  8.18 us
    all_to_all x1, starting transfers between devices, local(): lax.all_to_all(cotangent.T, 'row', split_axis=0, concat_axis=1, tiled=True)  7.26 us
  transfers between devices with their start and end apart: 2, of which 0 were waited for; matrix products, arithmetic and copies ran while one was open for 39% of the time, Pallas kernels for 0%

commit v1 on v0

--- a/solution.py
+++ b/solution.py
@@ -1,9 +1,14 @@
+import functools
+
 import jax
 import jax.numpy as jnp
 from jax import lax
+from jax.experimental import pallas as pl
+from jax.experimental.pallas import tpu as pltpu
 from jax.sharding import PartitionSpec as P
 
 BLOCK = 256
+CHUNK = 1024
 
 
 def tile_keep(block_mask, row_start, rows, col_start, cols):
@@ -21,7 +26,7 @@
     return jnp.dot(narrow, col_pick, preferred_element_type=jnp.float32).astype(jnp.bfloat16)
 
 
-def local(hidden, cotangent, weight_t, block_mask):
+def general(hidden, cotangent, weight_t, block_mask):
     feat_rows, hid_cols = weight_t.shape
     row_index = lax.axis_index("row")
     col_index = lax.axis_index("col")
@@ -33,15 +38,269 @@
         piece, kept, (((1,), (1,)), ((), ())), preferred_element_type=jnp.float32
     )
     grad = jnp.dot(cot_feat, piece, preferred_element_type=jnp.float32)
-    partial_out, grad = (part, grad)
-    output = lax.psum_scatter(partial_out, "col", scatter_dimension=0, tiled=True).astype(
-        jnp.bfloat16
+    output = lax.psum_scatter(part, "col", scatter_dimension=0, tiled=True).astype(jnp.bfloat16)
+    return output, grad * keep.astype(jnp.float32)
+
+
+def exchange(
+    n,
+    hidden_ref, cot_ref, weight_ref, mask_ref,
+    gathered, cot_feat, out_ref,
+    weight, total, other_part,
+    weight_sem, hid_send, hid_recv, cot_send, cot_recv, pair_send, pair_recv,
+):
+    rows, cols = hidden_ref.shape
+    feats = weight_ref.shape[0]
+    f_tiles = feats // BLOCK
+    chunks = cols // CHUNK
+    tiles = CHUNK // BLOCK
+    half_feats = feats // 2
+    tokens = n * rows
+    me = lax.axis_index("row")
+    core = lax.axis_index("col")
+    half = n // 2
+
+    side = lax.rem(me, 2)
+    spot = jnp.where(side == 0, me // 2, n - 1 - me // 2)
+
+    def row_of(place):
+        place = lax.rem(place + 2 * n, n)
+        return jnp.where(place < half, 2 * place, 2 * (n - 1 - place) + 1)
+
+    heads = [row_of(spot + 1), row_of(spot - 1)]
+
+    def span(c):
+        return pl.ds(c * CHUNK, CHUNK)
+
+    loads = []
+    for c in range(chunks):
+        load = pltpu.make_async_copy(
+            weight_ref.at[:, span(c)], weight.at[:, span(c)], weight_sem.at[c]
+        )
+        load.start()
+        loads.append(load)
+
+    barrier = pltpu.get_barrier_semaphore()
+    for d in range(1, n):
+        pl.semaphore_signal(
+            barrier, inc=1, device_id={"row": lax.rem(me + d, n)},
+            device_id_type=pl.DeviceIdType.MESH,
+        )
+    pl.semaphore_signal(
+        barrier, inc=1, device_id={"col": 1 - core}, device_id_type=pl.DeviceIdType.MESH
     )
-    weight_grad = grad * keep.astype(jnp.float32)
-    return (output, weight_grad)
+    pl.semaphore_wait(barrier, n)
+
+    def hop(way, h, c):
+        source = row_of(spot - (h - 1)) if way == 0 else row_of(spot + (h - 1))
+        here = gathered.at[source, :, span(c)]
+        return pltpu.make_async_remote_copy(
+            src_ref=hidden_ref.at[:, span(c)] if h == 1 else here,
+            dst_ref=here,
+            send_sem=hid_send.at[way, h - 1, c],
+            recv_sem=hid_recv.at[way, h - 1, c],
+            device_id={"row": heads[way]},
+            device_id_type=pl.DeviceIdType.MESH,
+        )
+
+    def arrival(way, h, c):
+        source = row_of(spot - h) if way == 0 else row_of(spot + h)
+        here = gathered.at[source, :, span(c)]
+        return pltpu.make_async_remote_copy(
+            src_ref=here,
+            dst_ref=here,
+            send_sem=hid_send.at[way, h - 1, c],
+            recv_sem=hid_recv.at[way, h - 1, c],
+            device_id={"row": heads[way]},
+            device_id_type=pl.DeviceIdType.MESH,
+        )
+
+    sent = []
+
+    def send(way, h, c):
+        copy = hop(way, h, c)
+        copy.start()
+        sent.append(copy)
+
+    ahead = min(2, chunks)
+    for c in range(ahead):
+        for way in range(2):
+            send(way, 1, c)
+
+    my_half = pl.ds(pl.multiple_of(core * half_feats, 128), half_feats)
+    cot_copies = []
+    for d in range(1, n):
+        to = lax.rem(me + d, n)
+        piece = pl.ds(pl.multiple_of(to * feats + core * half_feats, 128), half_feats)
+        copy = pltpu.make_async_remote_copy(
+            src_ref=cot_ref.at[:, piece],
+            dst_ref=cot_feat.at[me, :, my_half],
+            send_sem=cot_send.at[d - 1],
+            recv_sem=cot_recv.at[d - 1],
+            device_id={"row": to},
+            device_id_type=pl.DeviceIdType.MESH,
+        )
+        copy.start()
+        cot_copies.append(copy)
+    own = pl.ds(pl.multiple_of(me * feats + core * half_feats, 128), half_feats)
+    cot_feat[me, :, my_half] = cot_ref[:, own]
+    gathered[me, :, :] = hidden_ref[...]
+    total[...] = jnp.zeros_like(total)
+
+    def multiply(c):
+        loads[c].wait()
+        block = gathered[:, :, c * CHUNK:(c + 1) * CHUNK].reshape(tokens, CHUNK)
+        for f in range(f_tiles):
+            parts = []
+            for t in range(tiles):
+                factor = mask_ref[me * f_tiles + f, core * (chunks * tiles) + c * tiles + t]
+                factor = factor.astype(jnp.float32).astype(jnp.bfloat16)
+                parts.append(block[:, t * BLOCK:(t + 1) * BLOCK] * factor)
+            picked = jnp.concatenate(parts, axis=1)
+            lanes = slice(f * BLOCK, (f + 1) * BLOCK)
+            total[:, lanes] += lax.dot_general(
+                picked,
+                weight[lanes, c * CHUNK:(c + 1) * CHUNK],
+                (((1,), (1,)), ((), ())),
+                preferred_element_type=jnp.float32,
+            )
+
+    def ways(h, c):
+        return [0, 1] if h < half else [c % 2]
+
+    for t in range(chunks + half):
+        if t + ahead < chunks:
+            for way in range(2):
+                send(way, 1, t + ahead)
+        for h in range(1, half + 1):
+            c = t - (h - 1)
+            if 0 <= c < chunks:
+                for way in ways(h, c):
+                    arrival(way, h, c).wait_recv()
+                    if h < half and way in ways(h + 1, c):
+                        send(way, h + 1, c)
+        if t == half:
+            for copy in cot_copies:
+                copy.wait_recv()
+            mine = cot_feat.at[:, :, my_half]
+            cot_pair = pltpu.make_async_remote_copy(
+                src_ref=mine, dst_ref=mine,
+                send_sem=pair_send.at[0], recv_sem=pair_recv.at[0],
+                device_id={"col": 1 - core}, device_id_type=pl.DeviceIdType.MESH,
+            )
+            cot_pair.start()
+        c = t - (half - 1)
+        if 0 <= c < chunks:
+            multiply(c)
+
+    kept_rows = tokens // 2
+    pair = pltpu.make_async_remote_copy(
+        src_ref=total.at[pl.ds(pl.multiple_of((1 - core) * kept_rows, 8), kept_rows)],
+        dst_ref=other_part,
+        send_sem=pair_send.at[1], recv_sem=pair_recv.at[1],
+        device_id={"col": 1 - core}, device_id_type=pl.DeviceIdType.MESH,
+    )
+    pair.start()
+    for copy in sent:
+        copy.wait_send()
+    for copy in cot_copies:
+        copy.wait_send()
+    cot_pair.wait()
+    pair.wait()
+    mine = total[pl.ds(pl.multiple_of(core * kept_rows, 8), kept_rows), :]
+    out_ref[...] = (mine + other_part[...]).astype(out_ref.dtype)
+
+
+def outer(splits, gathered, cot_feat, mask_ref, grad_ref):
+    n, rows, cols = gathered.shape
+    tokens = n * rows
+    feats = cot_feat.shape[2]
+    f_tiles = feats // BLOCK
+    me = lax.axis_index("row")
+    core = lax.axis_index("col")
+    f = pl.program_id(0)
+    part = pl.program_id(1)
+    width = cols // splits
+    tiles = width // BLOCK
+    left = cot_feat[:, :, pl.ds(pl.multiple_of(f * BLOCK, BLOCK), BLOCK)].reshape(tokens, BLOCK)
+    for t in range(tiles):
+        k = part * tiles + t
+        factor = mask_ref[me * f_tiles + f, core * (tiles * splits) + k]
+        factor = factor.astype(jnp.float32).astype(jnp.bfloat16)
+        block = gathered[:, :, pl.ds(pl.multiple_of(k * BLOCK, BLOCK), BLOCK)]
+        grad_ref[:, t * BLOCK:(t + 1) * BLOCK] = lax.dot_general(
+            left,
+            block.reshape(tokens, BLOCK) * factor,
+            (((0,), (0,)), ((), ())),
+            preferred_element_type=jnp.float32,
+        )
+
+
+def tiled(n, hidden, cotangent, weight_t, block_mask):
+    rows, cols = hidden.shape
+    feats = weight_t.shape[0]
+    tokens = n * rows
+    half = n // 2
+    chunks = cols // CHUNK
+    vmem = pl.BlockSpec(memory_space=pltpu.VMEM)
+    smem = pl.BlockSpec(memory_space=pltpu.SMEM)
+    gathered, cot_feat, output = pl.pallas_call(
+        functools.partial(exchange, n),
+        out_shape=(
+            jax.ShapeDtypeStruct((n, rows, cols), jnp.bfloat16),
+            jax.ShapeDtypeStruct((n, rows, feats), jnp.bfloat16),
+            jax.ShapeDtypeStruct((tokens // 2, feats), jnp.bfloat16),
+        ),
+        in_specs=[vmem, vmem, pl.BlockSpec(memory_space=pl.ANY), smem],
+        out_specs=(vmem, vmem, vmem),
+        scratch_shapes=[
+            pltpu.VMEM((feats, cols), jnp.bfloat16),
+            pltpu.VMEM((tokens, feats), jnp.float32),
+            pltpu.VMEM((tokens // 2, feats), jnp.float32),
+            pltpu.SemaphoreType.DMA((chunks,)),
+            pltpu.SemaphoreType.DMA((2, half, chunks)),
+            pltpu.SemaphoreType.DMA((2, half, chunks)),
+            pltpu.SemaphoreType.DMA((n - 1,)),
+            pltpu.SemaphoreType.DMA((n - 1,)),
+            pltpu.SemaphoreType.DMA((2,)),
+            pltpu.SemaphoreType.DMA((2,)),
+        ],
+        compiler_params=pltpu.CompilerParams(
+            collective_id=0, has_side_effects=True, vmem_limit_bytes=40 * 1024 * 1024
+        ),
+        cost_estimate=pl.CostEstimate(
+            flops=2 * tokens * feats * cols,
+            bytes_accessed=2 * feats * cols,
+            transcendentals=0,
+        ),
+    )(hidden, cotangent, weight_t, block_mask)
+    splits = 4
+    grad = pl.pallas_call(
+        functools.partial(outer, splits),
+        grid=(feats // BLOCK, splits),
+        out_shape=jax.ShapeDtypeStruct((feats, cols), jnp.float32),
+        in_specs=[vmem, vmem, smem],
+        out_specs=pl.BlockSpec((BLOCK, cols // splits), lambda f, s: (f, s)),
+        compiler_params=pltpu.CompilerParams(vmem_limit_bytes=40 * 1024 * 1024),
+        cost_estimate=pl.CostEstimate(
+            flops=2 * tokens * feats * cols,
+            bytes_accessed=4 * feats * cols,
+            transcendentals=0,
+        ),
+    )(gathered, cot_feat, block_mask)
+    return output, grad
 
 
 def solution(mesh):
+    n = mesh.shape["row"]
+
+    def local(hidden, cotangent, weight_t, block_mask):
+        feats, cols = weight_t.shape
+        whole_tiles = feats % BLOCK == 0 and cols % CHUNK == 0
+        if whole_tiles and n % 2 == 0 and mesh.shape["col"] == 2:
+            return tiled(n, hidden, cotangent, weight_t, block_mask)
+        return general(hidden, cotangent, weight_t, block_mask)
+
     return jax.shard_map(
         local,
         mesh=mesh,

time: 92.8 us -> 52.3 us (0.56)
  Pallas kernels: 0 us -> 48.3 us
  matrix products: 36 us -> 0 us
  blocking collectives: 33.4 us -> 0 us
  between operations: 14.1 us -> 0.65 us
  starting transfers between devices: 7.3 us -> 0 us
  local copies, waits for them, and re-layouts: 0 us -> 3.14 us
  other arithmetic: 1.57 us -> 0 us
    pallas_call x0 -> x2, Pallas kernels: none -> 48.3 us  [the longest x1 33.6 us: tiled(): pl.pallas_call(functools.partial(exchange, n), out_shape=(jax.ShapeDtypeS...]
    dot_general x3 -> x0, matrix products: 36 us -> none  [the longest x1 15.5 us: local(): grad = jnp.dot(cot_feat, piece, preferred_element_type=jnp.float32)]
    all_gather x1 -> x0, blocking collectives: 33.4 us -> none  [local(): piece = lax.all_gather(hidden, 'row', axis=0, tiled=True)]
    all_to_all x1 -> x0, starting transfers between devices: 7.26 us -> none  [local(): lax.all_to_all(cotangent.T, 'row', split_axis=0, concat_axis=1, tiled=True)]
    unnamed x0 -> x7, local copies, waits for them, and re-layouts: none -> 3.14 us
    convert_element_type x1 -> x0, other arithmetic: 1.54 us -> none  [local(): lax.psum_scatter(partial_out, 'col', scatter_dimension=0, tiled=True)]
  transfers between devices with their start and end apart: 2 -> 0, of which waited for: 0 -> 0; matrix products, arithmetic and copies ran while one was open for 39% -> 0% of each run, Pallas kernels for 0% -> 0%
where the time goes in v1:
time: 52.3 us; the launch traced here: 52.1 us
  Pallas kernels  48.3 us (92%)
  local copies, waits for them, and re-layouts  3.14 us (6%)
  between operations  0.65 us (1%)
    pallas_call x1, Pallas kernels, tiled(): pl.pallas_call(functools.partial(exchange, n), out_shape=(jax.ShapeDtypeS...  33.6 us
    pallas_call x1, Pallas kernels, tiled(): pl.pallas_call(functools.partial(outer, splits), grid=(feats // BLOCK, sp...  14.7 us
    unnamed x7, local copies, waits for them, and re-layouts  3.14 us

profile of v1, /device:TPU:0, one launch (start us, length us, event | category | flops | bytes accessed | tf_op | source)
XLA Modules:
  0.0 52.1 jit_solution(2840427737444530096)
XLA Ops:
  0.6 0.0 copy-start
  0.6 0.9 %copy-done = bf16[8,8192]{1,0:T(8,128)(2,1)S(1)} copy-done((bf16[8,8192]{1,0:T(8,128)(2,1)S(1)}, bf16[8,8192]{1,0:T(8,128)(2,1)}, u32[]{:S(2)}) %copy-start) | copy-done | bytes 131096
  1.5 0.0 copy-start.1
  1.5 0.9 %copy-done.1 = bf16[8,7168]{1,0:T(8,128)(2,1)S(1)} copy-done((bf16[8,7168]{1,0:T(8,128)(2,1)S(1)}, bf16[8,7168]{1,0:T(8,128)(2,1)}, u32[]{:S(2)}) %copy-start.1) | copy-done | bytes 114712
  2.4 0.0 copy-start.2
  2.4 0.7 %copy-done.2 = s32[32,56]{1,0:T(8,128)S(1)} copy-done((s32[32,56]{1,0:T(8,128)S(1)}, s32[32,56]{1,0:T(8,128)}, u32[]{:S(2)}) %copy-start.2) | copy-done | bytes 7192
  3.2 33.6 %shard_map.59 = (bf16[8,8,7168]{2,1,0:T(8,128)(2,1)S(1)}, bf16[8,8,1024]{2,1,0:T(8,128)(2,1)S(1)}, bf16[32,1024]{1,0:T(8,128)(2,1)S(1)}) custom-call(bf16[8,7168]{1,0:T(8,128)(2,1)S(1)} %copy-done.1, bf16[8,8192]{1,0:T(8,128)(2,1)S(1)} %copy-done, bf16[1024,7168]{1,0:T(8,128)(2,1)} %weight_ref.1, s32[32,56]{1,0:T(8,128)S(1)} %copy-done.2), custom_call_target="tpu_custom_call" | custom-call | flops 939524096 | bytes 14680064 | tf_op jit(solution)/shard_map/pallas_call | solution.py:247
  36.7 14.7 %shard_map.60 = f32[1024,7168]{1,0:T(8,128)} custom-call(bf16[8,8,7168]{2,1,0:T(8,128)(2,1)S(1)} %get-tuple-element.6.gathered, bf16[8,8,1024]{2,1,0:T(8,128)(2,1)S(1)} %get-tuple-element.7.cot_feat, s32[32,56]{1,0:T(8,128)S(1)} %copy-done.2), custom_call_target="tpu_custom_call" | custom-call | flops 939524096 | bytes 29360128 | tf_op jit(solution)/shard_map/pallas_call | solution.py:278
  51.5 0.6 %copy.7 = bf16[32,1024]{1,0:T(8,128)(2,1)} copy(bf16[32,1024]{1,0:T(8,128)(2,1)S(1)} %get-tuple-element.10) | data formatting | bytes 131072
Async XLA Ops:
  0.6 0.9 %copy-start = (bf16[8,8192]{1,0:T(8,128)(2,1)S(1)}, bf16[8,8192]{1,0:T(8,128)(2,1)}, u32[]{:S(2)}) copy-start(bf16[8,8192]{1,0:T(8,128)(2,1)} %cot_ref.1) | copy-start | bytes 393220
  1.5 0.9 %copy-start.1 = (bf16[8,7168]{1,0:T(8,128)(2,1)S(1)}, bf16[8,7168]{1,0:T(8,128)(2,1)}, u32[]{:S(2)}) copy-start(bf16[8,7168]{1,0:T(8,128)(2,1)} %hidden_ref.1) | copy-start | bytes 344068
  2.4 0.7 %copy-start.2 = (s32[32,56]{1,0:T(8,128)S(1)}, s32[32,56]{1,0:T(8,128)}, u32[]{:S(2)}) copy-start(s32[32,56]{1,0:T(8,128)} %mask_ref.3) | copy-start | bytes 21508

commit v2 on v0

--- a/solution.py
+++ b/solution.py
@@ -1,9 +1,15 @@
+import functools
+
 import jax
 import jax.numpy as jnp
 from jax import lax
+from jax.experimental import pallas as pl
+from jax.experimental.pallas import tpu as pltpu
 from jax.sharding import PartitionSpec as P
 
 BLOCK = 256
+CHUNKS = 4
+HEIGHT = 128
 
 
 def tile_keep(block_mask, row_start, rows, col_start, cols):
@@ -21,7 +27,7 @@
     return jnp.dot(narrow, col_pick, preferred_element_type=jnp.float32).astype(jnp.bfloat16)
 
 
-def local(hidden, cotangent, weight_t, block_mask):
+def general(hidden, cotangent, weight_t, block_mask):
     feat_rows, hid_cols = weight_t.shape
     row_index = lax.axis_index("row")
     col_index = lax.axis_index("col")
@@ -33,15 +39,267 @@
         piece, kept, (((1,), (1,)), ((), ())), preferred_element_type=jnp.float32
     )
     grad = jnp.dot(cot_feat, piece, preferred_element_type=jnp.float32)
-    partial_out, grad = (part, grad)
-    output = lax.psum_scatter(partial_out, "col", scatter_dimension=0, tiled=True).astype(
-        jnp.bfloat16
+    output = lax.psum_scatter(part, "col", scatter_dimension=0, tiled=True).astype(jnp.bfloat16)
+    return output, grad * keep.astype(jnp.float32)
+
+
+def exchange(
+    n,
+    hidden_ref, cot_ref, weight_ref, mask_ref,
+    gathered, cot_feat, mask_out, out_ref,
+    weight, total, other_part, mask,
+    weight_sem, hid_send, hid_recv, cot_send, cot_recv, pair_send, pair_recv, own_sem,
+):
+    rows, cols = hidden_ref.shape
+    feats = weight_ref.shape[0]
+    f_tiles = feats // BLOCK
+    chunk = cols // CHUNKS
+    tiles = chunk // BLOCK
+    half_feats = feats // 2
+    tokens = n * rows
+    me = lax.axis_index("row")
+    core = lax.axis_index("col")
+    half = n // 2
+    mesh_id = pl.DeviceIdType.MESH
+
+    spot = jnp.where(lax.rem(me, 2) == 0, me // 2, n - 1 - me // 2)
+
+    def row_of(place):
+        place = lax.rem(place + n, n)
+        return jnp.where(place < half, 2 * place, 2 * (n - 1 - place) + 1)
+
+    places = [
+        [row_of(spot - back) for back in range(half + 1)],
+        [row_of(spot + back) for back in range(half + 1)],
+    ]
+    heads = [places[1][1], places[0][1]]
+
+    barrier = pltpu.get_barrier_semaphore()
+    for d in range(1, n):
+        pl.semaphore_signal(
+            barrier, inc=1, device_id={"row": lax.rem(me + d, n)}, device_id_type=mesh_id
+        )
+    pl.semaphore_signal(barrier, inc=1, device_id={"col": 1 - core}, device_id_type=mesh_id)
+
+    def span(c):
+        return pl.ds(c * chunk, chunk)
+
+    my_half = pl.ds(pl.multiple_of(core * half_feats, 128), half_feats)
+
+    def cot_piece(to):
+        return cot_ref.at[:, pl.ds(pl.multiple_of(to * feats + core * half_feats, 128), half_feats)]
+
+    pl.semaphore_wait(barrier, n)
+
+    def hop(way, h, c, back):
+        here = gathered.at[places[way][back], :, span(c)]
+        return pltpu.make_async_remote_copy(
+            src_ref=hidden_ref.at[:, span(c)] if back == 0 else here,
+            dst_ref=here,
+            send_sem=hid_send.at[way],
+            recv_sem=hid_recv.at[way, h - 1, c],
+            device_id={"row": heads[way]},
+            device_id_type=mesh_id,
+        )
+
+    for c in range(CHUNKS):
+        for way in range(2):
+            hop(way, 1, c, 0).start()
+
+    cot_copies = []
+    for d in range(1, n):
+        to = lax.rem(me + d, n)
+        copy = pltpu.make_async_remote_copy(
+            src_ref=cot_piece(to),
+            dst_ref=cot_feat.at[me, :, my_half],
+            send_sem=cot_send.at[d - 1],
+            recv_sem=cot_recv.at[d - 1],
+            device_id={"row": to},
+            device_id_type=mesh_id,
+        )
+        copy.start()
+        cot_copies.append(copy)
+    locals_ = [
+        pltpu.make_async_copy(hidden_ref, gathered.at[me], own_sem.at[0]),
+        pltpu.make_async_copy(cot_piece(me), cot_feat.at[me, :, my_half], own_sem.at[1]),
+        pltpu.make_async_copy(mask_ref, mask, own_sem.at[2]),
+        pltpu.make_async_copy(mask_ref, mask_out, own_sem.at[3]),
+    ]
+    for copy in locals_:
+        copy.start()
+    loads = []
+    for c in range(CHUNKS):
+        load = pltpu.make_async_copy(
+            weight_ref.at[:, span(c)], weight.at[:, span(c)], weight_sem.at[c]
+        )
+        load.start()
+        loads.append(load)
+    total[...] = jnp.zeros_like(total)
+
+    def last_way(c):
+        return 0 if c < CHUNKS // 2 else 1
+
+    for h in range(1, half):
+        for c in range(CHUNKS):
+            for way in range(2):
+                hop(way, h, c, h).wait_recv()
+                if h + 1 < half or last_way(c) == way:
+                    hop(way, h + 1, c, h).start()
+    for copy in locals_:
+        copy.wait()
+    for copy in cot_copies:
+        copy.wait_recv()
+    mine = cot_feat.at[:, :, my_half]
+    cot_pair = pltpu.make_async_remote_copy(
+        src_ref=mine, dst_ref=mine,
+        send_sem=pair_send.at[0], recv_sem=pair_recv.at[0],
+        device_id={"col": 1 - core}, device_id_type=mesh_id,
     )
-    weight_grad = grad * keep.astype(jnp.float32)
-    return (output, weight_grad)
+    cot_pair.start()
+
+    def multiply(c):
+        loads[c].wait()
+        block = gathered[:, :, c * chunk:(c + 1) * chunk].reshape(tokens, chunk)
+        for f in range(f_tiles):
+            parts = []
+            for t in range(tiles):
+                factor = mask[me * f_tiles + f, core * (CHUNKS * tiles) + c * tiles + t]
+                factor = factor.astype(jnp.float32).astype(jnp.bfloat16)
+                parts.append(block[:, t * BLOCK:(t + 1) * BLOCK] * factor)
+            picked = jnp.concatenate(parts, axis=1)
+            lanes = slice(f * BLOCK, (f + 1) * BLOCK)
+            total[:, lanes] += lax.dot_general(
+                picked,
+                weight[lanes, c * chunk:(c + 1) * chunk],
+                (((1,), (1,)), ((), ())),
+                preferred_element_type=jnp.float32,
+            )
+
+    for i in range(CHUNKS // 2):
+        for c in (i, i + CHUNKS // 2):
+            hop(last_way(c), half, c, half).wait_recv()
+            multiply(c)
+
+    kept_rows = tokens // 2
+    pair = pltpu.make_async_remote_copy(
+        src_ref=total.at[pl.ds(pl.multiple_of((1 - core) * kept_rows, 8), kept_rows)],
+        dst_ref=other_part,
+        send_sem=pair_send.at[1], recv_sem=pair_recv.at[1],
+        device_id={"col": 1 - core}, device_id_type=mesh_id,
+    )
+    pair.start()
+    for way in range(2):
+        all_sent = gathered.at[pl.ds(0, n - 1), :, pl.ds(0, cols // 2)]
+        pltpu.make_async_remote_copy(
+            src_ref=all_sent, dst_ref=all_sent,
+            send_sem=hid_send.at[way], recv_sem=hid_recv.at[way, 0, 0],
+            device_id={"row": heads[way]}, device_id_type=mesh_id,
+        ).wait_send()
+    for copy in cot_copies:
+        copy.wait_send()
+    cot_pair.wait()
+    pair.wait()
+    mine = total[pl.ds(pl.multiple_of(core * kept_rows, 8), kept_rows), :]
+    out_ref[...] = (mine + other_part[...]).astype(out_ref.dtype)
+
+
+def outer(gathered, cot_feat, mask_ref, grad_ref):
+    n, rows, cols = gathered.shape
+    tokens = n * rows
+    feats = cot_feat.shape[2]
+    f_tiles = feats // BLOCK
+    height = grad_ref.shape[0]
+    tiles = cols // BLOCK
+    me = lax.axis_index("row")
+    core = lax.axis_index("col")
+    step = pl.program_id(0)
+    f = step // (BLOCK // height)
+    left = cot_feat[:, :, pl.ds(pl.multiple_of(step * height, height), height)]
+    left = left.reshape(tokens, height)
+    for t in range(tiles):
+        factor = mask_ref[me * f_tiles + f, core * tiles + t]
+        factor = factor.astype(jnp.float32).astype(jnp.bfloat16)
+        lanes = slice(t * BLOCK, (t + 1) * BLOCK)
+        grad_ref[:, lanes] = lax.dot_general(
+            left,
+            gathered[:, :, lanes].reshape(tokens, BLOCK) * factor,
+            (((0,), (0,)), ((), ())),
+            preferred_element_type=jnp.float32,
+        )
+
+
+def grad_of(gathered, cot_feat, block_mask):
+    n, rows, cols = gathered.shape
+    feats = cot_feat.shape[2]
+    vmem = pl.BlockSpec(memory_space=pltpu.VMEM)
+    return pl.pallas_call(
+        outer,
+        grid=(feats // HEIGHT,),
+        out_shape=jax.ShapeDtypeStruct((feats, cols), jnp.float32),
+        in_specs=[vmem, vmem, pl.BlockSpec(memory_space=pltpu.SMEM)],
+        out_specs=pl.BlockSpec((HEIGHT, cols), lambda step: (step, 0)),
+        compiler_params=pltpu.CompilerParams(vmem_limit_bytes=40 * 1024 * 1024),
+        cost_estimate=pl.CostEstimate(
+            flops=2 * n * rows * feats * cols,
+            bytes_accessed=4 * feats * cols,
+            transcendentals=0,
+        ),
+    )(gathered, cot_feat, block_mask)
+
+
+def tiled(n, hidden, cotangent, weight_t, block_mask):
+    rows, cols = hidden.shape
+    feats = weight_t.shape[0]
+    tokens = n * rows
+    half = n // 2
+    vmem = pl.BlockSpec(memory_space=pltpu.VMEM)
+    hbm = pl.BlockSpec(memory_space=pltpu.HBM)
+    gathered, cot_feat, mask, output = pl.pallas_call(
+        functools.partial(exchange, n),
+        out_shape=(
+            jax.ShapeDtypeStruct((n, rows, cols), jnp.bfloat16),
+            jax.ShapeDtypeStruct((n, rows, feats), jnp.bfloat16),
+            jax.ShapeDtypeStruct(block_mask.shape, jnp.int32),
+            jax.ShapeDtypeStruct((tokens // 2, feats), jnp.bfloat16),
+        ),
+        in_specs=[hbm, hbm, hbm, hbm],
+        out_specs=(vmem, vmem, vmem, vmem),
+        scratch_shapes=[
+            pltpu.VMEM((feats, cols), jnp.bfloat16),
+            pltpu.VMEM((tokens, feats), jnp.float32),
+            pltpu.VMEM((tokens // 2, feats), jnp.float32),
+            pltpu.SMEM(block_mask.shape, jnp.int32),
+            pltpu.SemaphoreType.DMA((CHUNKS,)),
+            pltpu.SemaphoreType.DMA((2,)),
+            pltpu.SemaphoreType.DMA((2, half, CHUNKS)),
+            pltpu.SemaphoreType.DMA((n - 1,)),
+            pltpu.SemaphoreType.DMA((n - 1,)),
+            pltpu.SemaphoreType.DMA((2,)),
+            pltpu.SemaphoreType.DMA((2,)),
+            pltpu.SemaphoreType.DMA((4,)),
+        ],
+        compiler_params=pltpu.CompilerParams(
+            collective_id=0, has_side_effects=True, vmem_limit_bytes=40 * 1024 * 1024
+        ),
+        cost_estimate=pl.CostEstimate(
+            flops=2 * tokens * feats * cols,
+            bytes_accessed=2 * feats * cols,
+            transcendentals=0,
+        ),
+    )(hidden, cotangent, weight_t, block_mask)
+    return output, grad_of(gathered, cot_feat, mask)
 
 
 def solution(mesh):
+    n = mesh.shape["row"]
+
+    def local(hidden, cotangent, weight_t, block_mask):
+        feats, cols = weight_t.shape
+        whole_tiles = feats % BLOCK == 0 and cols % (CHUNKS * BLOCK) == 0
+        if whole_tiles and n % 2 == 0 and mesh.shape["col"] == 2:
+            return tiled(n, hidden, cotangent, weight_t, block_mask)
+        return general(hidden, cotangent, weight_t, block_mask)
+
     return jax.shard_map(
         local,
         mesh=mesh,

time: 92.8 us -> 40.7 us (0.44)
  Pallas kernels: 0 us -> 36.7 us
  matrix products: 36 us -> 0 us
  blocking collectives: 33.4 us -> 0 us
  between operations: 14.1 us -> 0.65 us
  starting transfers between devices: 7.3 us -> 0 us
  local copies, waits for them, and re-layouts: 0 us -> 3.14 us
  other arithmetic: 1.57 us -> 0 us
    pallas_call x0 -> x2, Pallas kernels: none -> 36.7 us  [the longest x1 24.6 us: tiled(): pl.pallas_call(functools.partial(exchange, n), out_shape=(jax.ShapeDtypeS...]
    dot_general x3 -> x0, matrix products: 36 us -> none  [the longest x1 15.5 us: local(): grad = jnp.dot(cot_feat, piece, preferred_element_type=jnp.float32)]
    all_gather x1 -> x0, blocking collectives: 33.4 us -> none  [local(): piece = lax.all_gather(hidden, 'row', axis=0, tiled=True)]
    all_to_all x1 -> x0, starting transfers between devices: 7.26 us -> none  [local(): lax.all_to_all(cotangent.T, 'row', split_axis=0, concat_axis=1, tiled=True)]
    unnamed x0 -> x7, local copies, waits for them, and re-layouts: none -> 3.14 us
    convert_element_type x1 -> x0, other arithmetic: 1.54 us -> none  [local(): lax.psum_scatter(partial_out, 'col', scatter_dimension=0, tiled=True)]
  transfers between devices with their start and end apart: 2 -> 0, of which waited for: 0 -> 0; matrix products, arithmetic and copies ran while one was open for 39% -> 0% of each run, Pallas kernels for 0% -> 0%
where the time goes in v2:
time: 40.7 us; the launch traced here: 40.5 us
  Pallas kernels  36.7 us (90%)
  local copies, waits for them, and re-layouts  3.14 us (8%)
  between operations  0.65 us (2%)
    pallas_call x1, Pallas kernels, tiled(): pl.pallas_call(functools.partial(exchange, n), out_shape=(jax.ShapeDtypeS...  24.6 us
    pallas_call x1, Pallas kernels, grad_of(): pl.pallas_call(outer, grid=(feats // HEIGHT,), out_shape=jax.ShapeDtypeSt...  12.1 us
    unnamed x7, local copies, waits for them, and re-layouts  3.14 us

profile of v2, /device:TPU:0, one launch (start us, length us, event | category | flops | bytes accessed | tf_op | source)
XLA Modules:
  0.0 40.5 jit_solution(17354605196076376590)
XLA Ops:
  0.6 0.0 copy-start
  0.6 0.9 %copy-done = bf16[8,8192]{1,0:T(8,128)(2,1)S(1)} copy-done((bf16[8,8192]{1,0:T(8,128)(2,1)S(1)}, bf16[8,8192]{1,0:T(8,128)(2,1)}, u32[]{:S(2)}) %copy-start) | copy-done | bytes 131096
  1.5 0.0 copy-start.1
  1.5 0.9 %copy-done.1 = bf16[8,7168]{1,0:T(8,128)(2,1)S(1)} copy-done((bf16[8,7168]{1,0:T(8,128)(2,1)S(1)}, bf16[8,7168]{1,0:T(8,128)(2,1)}, u32[]{:S(2)}) %copy-start.1) | copy-done | bytes 114712
  2.4 0.0 copy-start.2
  2.4 0.7 %copy-done.2 = s32[32,56]{1,0:T(8,128)S(1)} copy-done((s32[32,56]{1,0:T(8,128)S(1)}, s32[32,56]{1,0:T(8,128)}, u32[]{:S(2)}) %copy-start.2) | copy-done | bytes 7192
  3.2 24.6 %shard_map.59 = (bf16[8,8,7168]{2,1,0:T(8,128)(2,1)S(1)}, bf16[8,8,1024]{2,1,0:T(8,128)(2,1)S(1)}, s32[32,56]{1,0:T(8,128)S(1)}, bf16[32,1024]{1,0:T(8,128)(2,1)S(1)}) custom-call(bf16[8,7168]{1,0:T(8,128)(2,1)S(1)} %copy-done.1, bf16[8,8192]{1,0:T(8,128)(2,1)S(1)} %copy-done, bf16[1024,7168]{1,0:T(8,128)(2,1)} %weight_ref.1, s32[32,56]{1,0:T(8,128)S(1)} %copy-done.2), custom_call_target="tpu_custom_call" | custom-call | flops 939524096 | bytes 14680064 | tf_op jit(solution)/shard_map/pallas_call | solution.py:257
  27.8 12.1 %shard_map.60 = f32[1024,7168]{1,0:T(8,128)} custom-call(bf16[8,8,7168]{2,1,0:T(8,128)(2,1)S(1)} %get-tuple-element.7.gathered, bf16[8,8,1024]{2,1,0:T(8,128)(2,1)S(1)} %get-tuple-element.8.cot_feat, s32[32,56]{1,0:T(8,128)S(1)} %get-tuple-element.9.mask_ref), custom_call_target="tpu_custom_call" | custom-call | flops 939524096 | bytes 29360128 | tf_op jit(solution)/shard_map/pallas_call | solution.py:235
  39.8 0.6 %copy.7 = bf16[32,1024]{1,0:T(8,128)(2,1)} copy(bf16[32,1024]{1,0:T(8,128)(2,1)S(1)} %get-tuple-element.12) | data formatting | bytes 131072
Async XLA Ops:
  0.6 0.9 %copy-start = (bf16[8,8192]{1,0:T(8,128)(2,1)S(1)}, bf16[8,8192]{1,0:T(8,128)(2,1)}, u32[]{:S(2)}) copy-start(bf16[8,8192]{1,0:T(8,128)(2,1)} %cot_ref.1) | copy-start | bytes 393220
  1.5 0.9 %copy-start.1 = (bf16[8,7168]{1,0:T(8,128)(2,1)S(1)}, bf16[8,7168]{1,0:T(8,128)(2,1)}, u32[]{:S(2)}) copy-start(bf16[8,7168]{1,0:T(8,128)(2,1)} %hidden_ref.1) | copy-start | bytes 344068
  2.4 0.7 %copy-start.2 = (s32[32,56]{1,0:T(8,128)S(1)}, s32[32,56]{1,0:T(8,128)}, u32[]{:S(2)}) copy-start(s32[32,56]{1,0:T(8,128)} %mask_ref.1) | copy-start | bytes 21508

commit v3 on v2

--- a/solution.py
+++ b/solution.py
@@ -286,7 +286,12 @@
             bytes_accessed=2 * feats * cols,
             transcendentals=0,
         ),
-    )(hidden, cotangent, weight_t, block_mask)
+    )(
+        *(
+            pltpu.with_memory_space_constraint(array, pltpu.HBM)
+            for array in (hidden, cotangent, weight_t, block_mask)
+        )
+    )
     return output, grad_of(gathered, cot_feat, mask)
 
 

time: 40.7 us -> 38.4 us (0.943)
  local copies, waits for them, and re-layouts: 3.14 us -> 0.63 us
    unnamed x7 -> x1, local copies, waits for them, and re-layouts: 3.14 us -> 0.63 us
where the time goes in v3:
time: 38.4 us; the launch traced here: 38.2 us
  Pallas kernels  37 us (96%)
  between operations  0.64 us (2%)
  local copies, waits for them, and re-layouts  0.63 us (2%)
    pallas_call x1, Pallas kernels, tiled(): pl.pallas_call(functools.partial(exchange, n), out_shape=(jax.ShapeDtypeS...  24.9 us
    pallas_call x1, Pallas kernels, grad_of(): pl.pallas_call(outer, grid=(feats // HEIGHT,), out_shape=jax.ShapeDtypeSt...  12.1 us

profile of v3, /device:TPU:0, one launch (start us, length us, event | category | flops | bytes accessed | tf_op | source)
XLA Modules:
  0.0 38.2 jit_solution(357568725043901614)
XLA Ops:
  0.6 24.9 %shard_map.59 = (bf16[8,8,7168]{2,1,0:T(8,128)(2,1)S(1)}, bf16[8,8,1024]{2,1,0:T(8,128)(2,1)S(1)}, s32[32,56]{1,0:T(8,128)S(1)}, bf16[32,1024]{1,0:T(8,128)(2,1)S(1)}) custom-call(bf16[8,7168]{1,0:T(8,128)(2,1)} %hidden_ref.1, bf16[8,8192]{1,0:T(8,128)(2,1)} %cot_ref.1, bf16[1024,7168]{1,0:T(8,128)(2,1)} %weight_ref.1, s32[32,56]{1,0:T(8,128)} %mask_ref.1), custom_call_target="tpu_custom_call" | custom-call | flops 939524096 | bytes 14680064 | tf_op jit(solution)/shard_map/pallas_call | solution.py:257
  25.5 12.1 %shard_map.60 = f32[1024,7168]{1,0:T(8,128)} custom-call(bf16[8,8,7168]{2,1,0:T(8,128)(2,1)S(1)} %get-tuple-element.7.gathered, bf16[8,8,1024]{2,1,0:T(8,128)(2,1)S(1)} %get-tuple-element.8.cot_feat, s32[32,56]{1,0:T(8,128)S(1)} %get-tuple-element.9.mask_ref), custom_call_target="tpu_custom_call" | custom-call | flops 939524096 | bytes 29360128 | tf_op jit(solution)/shard_map/pallas_call | solution.py:235
  37.6 0.6 %copy.7 = bf16[32,1024]{1,0:T(8,128)(2,1)} copy(bf16[32,1024]{1,0:T(8,128)(2,1)S(1)} %get-tuple-element.12) | data formatting | bytes 131072

commit v4 on v3

--- a/solution.py
+++ b/solution.py
@@ -8,7 +8,7 @@
 from jax.sharding import PartitionSpec as P
 
 BLOCK = 256
-CHUNKS = 4
+CHUNKS = 14
 HEIGHT = 128
 
 

time: 38.4 us -> 39.1 us (1.018)
  Pallas kernels: 37 us -> 37.7 us
    pallas_call x1, Pallas kernels: 24.9 us -> 25.6 us  [tiled(): pl.pallas_call(functools.partial(exchange, n), out_shape=(jax.ShapeDtypeS...]
where the time goes in v4:
time: 39.1 us; the launch traced here: 39 us
  Pallas kernels  37.7 us (96%)
  between operations  0.64 us (2%)
  local copies, waits for them, and re-layouts  0.63 us (2%)
    pallas_call x1, Pallas kernels, tiled(): pl.pallas_call(functools.partial(exchange, n), out_shape=(jax.ShapeDtypeS...  25.6 us
    pallas_call x1, Pallas kernels, grad_of(): pl.pallas_call(outer, grid=(feats // HEIGHT,), out_shape=jax.ShapeDtypeSt...  12.1 us

profile of v4, /device:TPU:0, one launch (start us, length us, event | category | flops | bytes accessed | tf_op | source)
XLA Modules:
  0.0 39.0 jit_solution(11001862053808155835)
XLA Ops:
  0.6 25.6 %shard_map.59 = (bf16[8,8,7168]{2,1,0:T(8,128)(2,1)S(1)}, bf16[8,8,1024]{2,1,0:T(8,128)(2,1)S(1)}, s32[32,56]{1,0:T(8,128)S(1)}, bf16[32,1024]{1,0:T(8,128)(2,1)S(1)}) custom-call(bf16[8,7168]{1,0:T(8,128)(2,1)} %hidden_ref.1, bf16[8,8192]{1,0:T(8,128)(2,1)} %cot_ref.1, bf16[1024,7168]{1,0:T(8,128)(2,1)} %weight_ref.1, s32[32,56]{1,0:T(8,128)} %mask_ref.1), custom_call_target="tpu_custom_call" | custom-call | flops 939524096 | bytes 14680064 | tf_op jit(solution)/shard_map/pallas_call | solution.py:257
  26.3 12.1 %shard_map.60 = f32[1024,7168]{1,0:T(8,128)} custom-call(bf16[8,8,7168]{2,1,0:T(8,128)(2,1)S(1)} %get-tuple-element.7.gathered, bf16[8,8,1024]{2,1,0:T(8,128)(2,1)S(1)} %get-tuple-element.8.cot_feat, s32[32,56]{1,0:T(8,128)S(1)} %get-tuple-element.9.mask_ref), custom_call_target="tpu_custom_call" | custom-call | flops 939524096 | bytes 29360128 | tf_op jit(solution)/shard_map/pallas_call | solution.py:235
  38.3 0.6 %copy.7 = bf16[32,1024]{1,0:T(8,128)(2,1)} copy(bf16[32,1024]{1,0:T(8,128)(2,1)S(1)} %get-tuple-element.12) | data formatting | bytes 131072
